TPU v7x, 32 devices: a whole 2x2x4 slice. The times are simulated.
32 devices in a mesh: lat: 4 (over x, core), lon: 8 (over z, y).
Axes of the slice: x: 2, y: 2, z: 4, core: 2. Of those that a mesh axis runs over, the one named last changes fastest.
Arguments:
- initial_state: float32 [4, 8, 64, 256], P('lat', 'lon'), may hold values from -6 to 6
- initial_reservoir: bfloat16 [4, 8, 64, 2048], P('lat', 'lon'), may hold values from -0.8984375 to 0.8984375
- coupling: bfloat16 [4, 8, 16, 4, 128, 128], P('lat', 'lon'), may hold values from -0.1875 to 0.1875
- input_weight: bfloat16 [4, 8, 16, 128, 128], P('lat', 'lon'), may hold values from -0.5 to 0.5
- readout: bfloat16 [4, 8, 2048, 256], P('lat', 'lon'), may hold values from -0.125 to 0.125
- intersection: int32 [4, 8, 2, 4], P('lat', 'lon'), may hold values from -1 to 7, as said below
Outputs:
- forecast: float32 [8, 4, 8, 64, 256], P(None, 'lat', 'lon')
Inputs may be any that keep to these rules, and one draw needn't show every extreme that they name: `intersection`: each list holds distinct point numbers in its first slots and -1 in the rest, with one or more live slots; the north lists of band 0 and the south lists of the last band hold only -1; in longitude sector 0 every list that is not a polar one has all four slots live.
All inputs are finite; a program needn't handle non-finite values.
Results may differ from a plain program's by a relative error of at most 0.018.
Values may be sent and summed in bfloat16 or wider, within the bound.
A program may use at most 64 MiB of HBM per device.

v0:
```python
import jax
import jax.numpy as jnp
import numpy as np
from jax import lax
from jax.sharding import PartitionSpec as P

VARS = 32
LATR = 4
LONC = 2
OV = 4
STEPS = 8
PTS = 8


def with_halo(value, sides, width):
    for axis, dim in sides:
        peers, length = (lax.axis_size(axis), value.shape[dim])
        up = [(i, (i + 1) % peers) for i in range(peers)]
        down = [(j, i) for i, j in up]
        last = lax.slice_in_dim(value, length - width, length, axis=dim)
        initial = lax.slice_in_dim(value, 0, width, axis=dim)
        before = lax.ppermute(last, axis, up)
        after = lax.ppermute(initial, axis, down)
        value = jnp.concatenate([before, value, after], axis=dim)
    return value


def shifted(value, axis, by):
    peers = lax.axis_size(axis)
    pairs = [(i, i + by) for i in range(peers) if 0 <= i + by < peers]
    return lax.ppermute(value, axis, pairs)


def select_points(source, slot_list):
    members = source.shape[0]
    points = source.reshape(members, PTS, VARS)
    onehot = (slot_list[:, None] == jnp.arange(PTS, dtype=jnp.int32)[None, :]).astype(jnp.bfloat16)
    picked = jnp.einsum("sp,mpv->msv", onehot, points, preferred_element_type=jnp.float32)
    return picked.astype(jnp.bfloat16).reshape(members, OV * VARS)


def per_device(initial_state, initial_reservoir, coupling, input_weight, readout, intersection):
    current = initial_state[0, 0]
    reservoir = initial_reservoir[0, 0]
    block_weight = coupling[0, 0]
    entry_weight = input_weight[0, 0]
    read_weight = readout[0, 0]
    lists = intersection[0, 0]
    members = current.shape[0]
    nodes = reservoir.shape[1]
    res_blocks = block_weight.shape[0]
    links = block_weight.shape[1]
    breadth = block_weight.shape[2]
    in_blocks = (current.shape[1] + 2 * LATR * VARS + 2 * OV * VARS) // breadth
    linked = (np.arange(res_blocks)[:, None] + np.arange(links)[None, :]) % res_blocks
    block_index = np.arange(res_blocks) % in_blocks
    even_nodes = jnp.arange(nodes) % 2 == 0
    outputs = []
    for moment in range(STEPS):
        rounded = current.astype(jnp.bfloat16)
        blocks = reservoir.reshape(members, res_blocks, breadth)
        activation = jnp.einsum(
            "mbki,bkio->mbo", blocks[:, linked], block_weight, preferred_element_type=jnp.float32
        )
        columns = rounded.reshape(members, LONC, LATR * VARS)
        padded = with_halo(columns, (("lon", 1),), 1)
        west_col = padded[:, 0]
        east_col = padded[:, -1]
        from_north = shifted(rounded, "lat", 1)
        from_south = shifted(rounded, "lat", -1)
        north_part = select_points(from_north, lists[0])
        south_part = select_points(from_south, lists[1])
        inputs = jnp.concatenate([rounded, west_col, east_col, north_part, south_part], axis=-1)
        chosen = inputs.reshape(members, in_blocks, breadth)[:, block_index]
        activation = activation + jnp.einsum(
            "mbi,bio->mbo", chosen, entry_weight, preferred_element_type=jnp.float32
        )
        reservoir = jnp.tanh(activation).astype(jnp.bfloat16).reshape(members, nodes)
        widened = reservoir.astype(jnp.float32)
        features = jnp.where(even_nodes, widened * widened, widened).astype(jnp.bfloat16)
        current = jnp.dot(features, read_weight, preferred_element_type=jnp.float32)
        outputs.append(current)
    return jnp.stack(outputs)[:, None, None]


def solution(mesh):
    in_specs = (
        P("lat", "lon", None, None),
        P("lat", "lon", None, None),
        P("lat", "lon", None, None, None, None),
        P("lat", "lon", None, None, None),
        P("lat", "lon", None, None),
        P("lat", "lon", None, None),
    )
    out_specs = P(None, "lat", "lon", None, None)
    return jax.shard_map(
        per_device, mesh=mesh, in_specs=in_specs, out_specs=out_specs, check_vma=False
    )
```

profile of v0, /device:TPU:30, one launch (start us, length us, event | category | flops | bytes accessed | tf_op | source)
XLA Modules:
  0.0 197.6 jit_solution(7540935760107519488)
XLA Ops:
  1.1 1.9 collective-permute-start.2
  3.0 3.6 %collective-permute-start.3 = (bf16[64,256]{0,1:T(8,128)(2,1)S(1)}, bf16[64,256]{0,1:T(8,128)(2,1)S(1)}, u32[]{:S(2)}, u32[]{:S(2)}) collective-permute-start(bf16[64,256]{0,1:T(8,128)(2,1)S(1)} %bitcast.445), channel_id=1, source_target_pairs={{8,0},{16,8},{24,16},{9,1},{17,9},{25,17},{10,2},{18,10},{26,18},{... | collective-permute-start | bytes 98312 | tf_op jit(solution)/shard_map/ppermute | solution.py:31
  7.5 1.9 collective-permute-start.1
  13.6 1.8 fusion.16
  23.9 2.1 %constant_dynamic-update-slice_fusion.46 = (f32[8,64,256]{2,1,0:T(8,128)}, bf16[64,256]{1,0:T(8,128)(2,1)S(1)}) fusion(bf16[1,1,2048,256]{3,2,1,0:T(8,128)(2,1)} %param.28, bf16[64,16,128]{2,0,1:T(8,128)(2,1)S(1)} %fusion.64, pred[16,128]{1,0:T(8,128)(4,1)S(1)} %copy-done.5), kind=kOutput, calls=%fused_computation.231 | convolution fusion | flops 67649536 | bytes 1411072 | tf_op jit(solution)/shard_map/dot_general | solution.py:81
  26.1 1.9 collective-permute-start.6
  28.0 3.6 %collective-permute-start.7 = (bf16[64,256]{1,0:T(8,128)(2,1)S(1)}, bf16[64,256]{1,0:T(8,128)(2,1)S(1)}, u32[]{:S(2)}, u32[]{:S(2)}) collective-permute-start(bf16[64,256]{1,0:T(8,128)(2,1)S(1)} %get-tuple-element.18), channel_id=1, source_target_pairs={{8,0},{16,8},{24,16},{9,1},{17,9},{25,17},{10,2},{18,10},{26,18},{... | collective-permute-start | bytes 98312 | tf_op jit(solution)/shard_map/ppermute | solution.py:31
  31.8 2.9 %collective-permute-start.4 = (bf16[64,1,128]{2,0,1:T(8,128)(2,1)S(1)}, bf16[64,1,128]{2,0,1:T(8,128)(2,1)S(1)}, u32[]{:S(2)}, u32[]{:S(2)}) collective-permute-start(bf16[64,1,128]{2,0,1:T(8,128)(2,1)S(1)} %copy.254), channel_id=1, source_target_pairs={{0,1},{1,2},{2,3},{3,4},{4,5},{5,6},{6,7},{7,0},{8,9},{9,10},{10,1... | collective-permute-start | bytes 49160 | tf_op jit(solution)/shard_map/ppermute | solution.py:22
  34.7 1.7 fusion.19
  36.5 6.4 %collective-permute-done.5 = bf16[64,1,128]{2,0,1:T(8,128)(2,1)S(1)} collective-permute-done((bf16[64,1,128]{2,0,1:T(8,128)(2,1)S(1)}, bf16[64,1,128]{2,0,1:T(8,128)(2,1)S(1)}, u32[]{:S(2)}, u32[]{:S(2)}) %collective-permute-start.5) | collective-permute-done | bytes 16416 | tf_op jit(solution)/shard_map/ppermute | solution.py:23
  50.3 2.1 %constant_dynamic-update-slice_fusion.45 = (f32[8,64,256]{2,1,0:T(8,128)}, bf16[64,256]{1,0:T(8,128)(2,1)S(1)}) fusion(f32[8,64,256]{2,1,0:T(8,128)} %get-tuple-element.37, bf16[1,1,2048,256]{3,2,1,0:T(8,128)(2,1)} %param.28, bf16[64,16,128]{2,0,1:T(8,128)(2,1)S(1)} %fusion.63, pred[16,128]{1,0:T(8,128)(4,1)S(1)} %copy-done.5), kind=kOutput, calls=%fused_computation.230 | convolution fusion | flops 67649536 | bytes 1411072 | tf_op jit(solution)/shard_map/dot_general | solution.py:81
  53.1 1.9 collective-permute-start.10
  55.0 3.6 %collective-permute-start.11 = (bf16[64,256]{1,0:T(8,128)(2,1)S(1)}, bf16[64,256]{1,0:T(8,128)(2,1)S(1)}, u32[]{:S(2)}, u32[]{:S(2)}) collective-permute-start(bf16[64,256]{1,0:T(8,128)(2,1)S(1)} %get-tuple-element.16), channel_id=1, source_target_pairs={{8,0},{16,8},{24,16},{9,1},{17,9},{25,17},{10,2},{18,10},{26,18},{... | collective-permute-start | bytes 98312 | tf_op jit(solution)/shard_map/ppermute | solution.py:31
  58.8 1.7 fusion.22
  60.5 2.1 %collective-permute-start.9 = (bf16[64,1,128]{2,0,1:T(8,128)(2,1)S(1)}, bf16[64,1,128]{2,0,1:T(8,128)(2,1)S(1)}, u32[]{:S(2)}, u32[]{:S(2)}) collective-permute-start(bf16[64,1,128]{2,0,1:T(8,128)(2,1)S(1)} %copy.257), channel_id=1, source_target_pairs={{1,0},{2,1},{3,2},{4,3},{5,4},{6,5},{7,6},{0,7},{9,8},{10,9},{11,1... | collective-permute-start | bytes 49160 | tf_op jit(solution)/shard_map/ppermute | solution.py:23
  63.2 3.8 %collective-permute-done.9 = bf16[64,1,128]{2,0,1:T(8,128)(2,1)S(1)} collective-permute-done((bf16[64,1,128]{2,0,1:T(8,128)(2,1)S(1)}, bf16[64,1,128]{2,0,1:T(8,128)(2,1)S(1)}, u32[]{:S(2)}, u32[]{:S(2)}) %collective-permute-start.9) | collective-permute-done | bytes 16416 | tf_op jit(solution)/shard_map/ppermute | solution.py:23
  73.3 1.7 gather_fusion.6
  75.0 2.1 %constant_dynamic-update-slice_fusion.44 = (f32[8,64,256]{2,1,0:T(8,128)}, bf16[64,256]{1,0:T(8,128)(2,1)S(1)}) fusion(f32[8,64,256]{2,1,0:T(8,128)} %get-tuple-element.39, bf16[1,1,2048,256]{3,2,1,0:T(8,128)(2,1)} %param.28, bf16[64,16,128]{2,0,1:T(8,128)(2,1)S(1)} %fusion.62, pred[16,128]{1,0:T(8,128)(4,1)S(1)} %copy-done.5), kind=kOutput, calls=%fused_computation.229 | convolution fusion | flops 67649536 | bytes 1411072 | tf_op jit(solution)/shard_map/dot_general | solution.py:81
  77.8 1.9 collective-permute-start.14
  79.7 3.6 %collective-permute-start.15 = (bf16[64,256]{1,0:T(8,128)(2,1)S(1)}, bf16[64,256]{1,0:T(8,128)(2,1)S(1)}, u32[]{:S(2)}, u32[]{:S(2)}) collective-permute-start(bf16[64,256]{1,0:T(8,128)(2,1)S(1)} %get-tuple-element.14), channel_id=1, source_target_pairs={{8,0},{16,8},{24,16},{9,1},{17,9},{25,17},{10,2},{18,10},{26,18},{... | collective-permute-start | bytes 98312 | tf_op jit(solution)/shard_map/ppermute | solution.py:31
  83.5 1.7 fusion.25
  85.2 2.1 %collective-permute-start.13 = (bf16[64,1,128]{2,0,1:T(8,128)(2,1)S(1)}, bf16[64,1,128]{2,0,1:T(8,128)(2,1)S(1)}, u32[]{:S(2)}, u32[]{:S(2)}) collective-permute-start(bf16[64,1,128]{2,0,1:T(8,128)(2,1)S(1)} %copy.259), channel_id=1, source_target_pairs={{1,0},{2,1},{3,2},{4,3},{5,4},{6,5},{7,6},{0,7},{9,8},{10,9},{11,1... | collective-permute-start | bytes 49160 | tf_op jit(solution)/shard_map/ppermute | solution.py:23
  87.9 3.8 %collective-permute-done.13 = bf16[64,1,128]{2,0,1:T(8,128)(2,1)S(1)} collective-permute-done((bf16[64,1,128]{2,0,1:T(8,128)(2,1)S(1)}, bf16[64,1,128]{2,0,1:T(8,128)(2,1)S(1)}, u32[]{:S(2)}, u32[]{:S(2)}) %collective-permute-start.13) | collective-permute-done | bytes 16416 | tf_op jit(solution)/shard_map/ppermute | solution.py:23
  99.7 2.1 %constant_dynamic-update-slice_fusion.43 = (f32[8,64,256]{2,1,0:T(8,128)}, bf16[64,256]{1,0:T(8,128)(2,1)S(1)}) fusion(f32[8,64,256]{2,1,0:T(8,128)} %get-tuple-element.41, bf16[1,1,2048,256]{3,2,1,0:T(8,128)(2,1)} %param.28, bf16[64,16,128]{2,0,1:T(8,128)(2,1)S(1)} %fusion.61, pred[16,128]{1,0:T(8,128)(4,1)S(1)} %copy-done.5), kind=kOutput, calls=%fused_computation.228 | convolution fusion | flops 67649536 | bytes 1411072 | tf_op jit(solution)/shard_map/dot_general | solution.py:81
  102.5 1.9 collective-permute-start.18
  104.4 3.6 %collective-permute-start.19 = (bf16[64,256]{1,0:T(8,128)(2,1)S(1)}, bf16[64,256]{1,0:T(8,128)(2,1)S(1)}, u32[]{:S(2)}, u32[]{:S(2)}) collective-permute-start(bf16[64,256]{1,0:T(8,128)(2,1)S(1)} %get-tuple-element.12), channel_id=1, source_target_pairs={{8,0},{16,8},{24,16},{9,1},{17,9},{25,17},{10,2},{18,10},{26,18},{... | collective-permute-start | bytes 98312 | tf_op jit(solution)/shard_map/ppermute | solution.py:31
  108.2 1.7 fusion.28
  110.0 2.1 %collective-permute-start.17 = (bf16[64,1,128]{2,0,1:T(8,128)(2,1)S(1)}, bf16[64,1,128]{2,0,1:T(8,128)(2,1)S(1)}, u32[]{:S(2)}, u32[]{:S(2)}) collective-permute-start(bf16[64,1,128]{2,0,1:T(8,128)(2,1)S(1)} %copy.261), channel_id=1, source_target_pairs={{1,0},{2,1},{3,2},{4,3},{5,4},{6,5},{7,6},{0,7},{9,8},{10,9},{11,1... | collective-permute-start | bytes 49160 | tf_op jit(solution)/shard_map/ppermute | solution.py:23
  112.6 3.8 %collective-permute-done.17 = bf16[64,1,128]{2,0,1:T(8,128)(2,1)S(1)} collective-permute-done((bf16[64,1,128]{2,0,1:T(8,128)(2,1)S(1)}, bf16[64,1,128]{2,0,1:T(8,128)(2,1)S(1)}, u32[]{:S(2)}, u32[]{:S(2)}) %collective-permute-start.17) | collective-permute-done | bytes 16416 | tf_op jit(solution)/shard_map/ppermute | solution.py:23
  124.4 2.1 %constant_dynamic-update-slice_fusion.42 = (f32[8,64,256]{2,1,0:T(8,128)}, bf16[64,256]{1,0:T(8,128)(2,1)S(1)}) fusion(f32[8,64,256]{2,1,0:T(8,128)} %get-tuple-element.43, bf16[1,1,2048,256]{3,2,1,0:T(8,128)(2,1)} %param.28, bf16[64,16,128]{2,0,1:T(8,128)(2,1)S(1)} %fusion.60, pred[16,128]{1,0:T(8,128)(4,1)S(1)} %copy-done.5), kind=kOutput, calls=%fused_computation.227 | convolution fusion | flops 67649536 | bytes 1411072 | tf_op jit(solution)/shard_map/dot_general | solution.py:81
  127.2 1.9 collective-permute-start.22
  129.1 3.6 %collective-permute-start.23 = (bf16[64,256]{1,0:T(8,128)(2,1)S(1)}, bf16[64,256]{1,0:T(8,128)(2,1)S(1)}, u32[]{:S(2)}, u32[]{:S(2)}) collective-permute-start(bf16[64,256]{1,0:T(8,128)(2,1)S(1)} %get-tuple-element.10), channel_id=1, source_target_pairs={{8,0},{16,8},{24,16},{9,1},{17,9},{25,17},{10,2},{18,10},{26,18},{... | collective-permute-start | bytes 98312 | tf_op jit(solution)/shard_map/ppermute | solution.py:31
  132.9 1.7 fusion.31
  134.7 2.1 %collective-permute-start.21 = (bf16[64,1,128]{2,0,1:T(8,128)(2,1)S(1)}, bf16[64,1,128]{2,0,1:T(8,128)(2,1)S(1)}, u32[]{:S(2)}, u32[]{:S(2)}) collective-permute-start(bf16[64,1,128]{2,0,1:T(8,128)(2,1)S(1)} %copy.263), channel_id=1, source_target_pairs={{1,0},{2,1},{3,2},{4,3},{5,4},{6,5},{7,6},{0,7},{9,8},{10,9},{11,1... | collective-permute-start | bytes 49160 | tf_op jit(solution)/shard_map/ppermute | solution.py:23
  137.3 3.8 %collective-permute-done.21 = bf16[64,1,128]{2,0,1:T(8,128)(2,1)S(1)} collective-permute-done((bf16[64,1,128]{2,0,1:T(8,128)(2,1)S(1)}, bf16[64,1,128]{2,0,1:T(8,128)(2,1)S(1)}, u32[]{:S(2)}, u32[]{:S(2)}) %collective-permute-start.21) | collective-permute-done | bytes 16416 | tf_op jit(solution)/shard_map/ppermute | solution.py:23
  149.1 2.1 %constant_dynamic-update-slice_fusion.41 = (f32[8,64,256]{2,1,0:T(8,128)}, bf16[64,256]{1,0:T(8,128)(2,1)S(1)}) fusion(f32[8,64,256]{2,1,0:T(8,128)} %get-tuple-element.45, bf16[1,1,2048,256]{3,2,1,0:T(8,128)(2,1)} %param.28, bf16[64,16,128]{2,0,1:T(8,128)(2,1)S(1)} %fusion.59, pred[16,128]{1,0:T(8,128)(4,1)S(1)} %copy-done.5), kind=kOutput, calls=%fused_computation.226 | convolution fusion | flops 67649536 | bytes 1411072 | tf_op jit(solution)/shard_map/dot_general | solution.py:81
  151.9 1.9 collective-permute-start.26
  153.8 3.6 %collective-permute-start.27 = (bf16[64,256]{1,0:T(8,128)(2,1)S(1)}, bf16[64,256]{1,0:T(8,128)(2,1)S(1)}, u32[]{:S(2)}, u32[]{:S(2)}) collective-permute-start(bf16[64,256]{1,0:T(8,128)(2,1)S(1)} %get-tuple-element.8), channel_id=1, source_target_pairs={{8,0},{16,8},{24,16},{9,1},{17,9},{25,17},{10,2},{18,10},{26,18},{... | collective-permute-start | bytes 98312 | tf_op jit(solution)/shard_map/ppermute | solution.py:31
  157.8 1.7 fusion.34
  159.5 2.1 %collective-permute-start.25 = (bf16[64,1,128]{2,0,1:T(8,128)(2,1)S(1)}, bf16[64,1,128]{2,0,1:T(8,128)(2,1)S(1)}, u32[]{:S(2)}, u32[]{:S(2)}) collective-permute-start(bf16[64,1,128]{2,0,1:T(8,128)(2,1)S(1)} %copy.265), channel_id=1, source_target_pairs={{1,0},{2,1},{3,2},{4,3},{5,4},{6,5},{7,6},{0,7},{9,8},{10,9},{11,1... | collective-permute-start | bytes 49160 | tf_op jit(solution)/shard_map/ppermute | solution.py:23
  162.2 3.8 %collective-permute-done.25 = bf16[64,1,128]{2,0,1:T(8,128)(2,1)S(1)} collective-permute-done((bf16[64,1,128]{2,0,1:T(8,128)(2,1)S(1)}, bf16[64,1,128]{2,0,1:T(8,128)(2,1)S(1)}, u32[]{:S(2)}, u32[]{:S(2)}) %collective-permute-start.25) | collective-permute-done | bytes 16416 | tf_op jit(solution)/shard_map/ppermute | solution.py:23
  174.0 2.1 %constant_dynamic-update-slice_fusion.40 = (f32[8,64,256]{2,1,0:T(8,128)}, bf16[64,256]{1,0:T(8,128)(2,1)S(1)}) fusion(f32[8,64,256]{2,1,0:T(8,128)} %get-tuple-element.47, bf16[1,1,2048,256]{3,2,1,0:T(8,128)(2,1)} %param.28, bf16[64,16,128]{2,0,1:T(8,128)(2,1)S(1)} %fusion.58, pred[16,128]{1,0:T(8,128)(4,1)S(1)} %copy-done.5), kind=kOutput, calls=%fused_computation.225 | convolution fusion | flops 67649536 | bytes 1411072 | tf_op jit(solution)/shard_map/dot_general | solution.py:81
  176.8 1.9 collective-permute-start.30
  178.7 3.6 %collective-permute-start.31 = (bf16[64,256]{1,0:T(8,128)(2,1)S(1)}, bf16[64,256]{1,0:T(8,128)(2,1)S(1)}, u32[]{:S(2)}, u32[]{:S(2)}) collective-permute-start(bf16[64,256]{1,0:T(8,128)(2,1)S(1)} %get-tuple-element.6), channel_id=1, source_target_pairs={{8,0},{16,8},{24,16},{9,1},{17,9},{25,17},{10,2},{18,10},{26,18},{... | collective-permute-start | bytes 98312 | tf_op jit(solution)/shard_map/ppermute | solution.py:31
  182.5 1.7 fusion.37
  184.3 2.1 %collective-permute-start.29 = (bf16[64,1,128]{2,0,1:T(8,128)(2,1)S(1)}, bf16[64,1,128]{2,0,1:T(8,128)(2,1)S(1)}, u32[]{:S(2)}, u32[]{:S(2)}) collective-permute-start(bf16[64,1,128]{2,0,1:T(8,128)(2,1)S(1)} %copy.267), channel_id=1, source_target_pairs={{1,0},{2,1},{3,2},{4,3},{5,4},{6,5},{7,6},{0,7},{9,8},{10,9},{11,1... | collective-permute-start | bytes 49160 | tf_op jit(solution)/shard_map/ppermute | solution.py:23
  186.9 3.8 %collective-permute-done.29 = bf16[64,1,128]{2,0,1:T(8,128)(2,1)S(1)} collective-permute-done((bf16[64,1,128]{2,0,1:T(8,128)(2,1)S(1)}, bf16[64,1,128]{2,0,1:T(8,128)(2,1)S(1)}, u32[]{:S(2)}, u32[]{:S(2)}) %collective-permute-start.29) | collective-permute-done | bytes 16416 | tf_op jit(solution)/shard_map/ppermute | solution.py:23
  195.4 2.2 %fusion.65 = f32[8,64,256]{2,1,0:T(8,128)} fusion(f32[8,64,256]{2,1,0:T(8,128)} %get-tuple-element.49, bf16[1,1,2048,256]{3,2,1,0:T(8,128)(2,1)} %param.28, bf16[16,8,8,128]{3,2,1,0:T(8,128)(2,1)S(1)} %fusion.98), kind=kOutput, calls=%fused_computation.74 | convolution fusion | flops 67108864 | bytes 1376256 | tf_op jit(solution)/shard_map/dot_general | solution.py:81
  (211 shorter events, 72.9 us)
Async XLA Ops:
  0.0 13.6 %copy-start = (bf16[1,1,16,4,128,128]{5,4,3,2,1,0:T(8,128)(2,1)S(1)}, bf16[1,1,16,4,128,128]{5,4,3,2,1,0:T(8,128)(2,1)}, u32[]{:S(2)}) copy-start(bf16[1,1,16,4,128,128]{5,4,3,2,1,0:T(8,128)(2,1)} %param.26) | copy-start | bytes 6291460
  1.1 16.4 %collective-permute-start.2 = (bf16[64,256]{0,1:T(8,128)(2,1)S(1)}, bf16[64,256]{0,1:T(8,128)(2,1)S(1)}, u32[]{:S(2)}, u32[]{:S(2)}) collective-permute-start(bf16[64,256]{0,1:T(8,128)(2,1)S(1)} %bitcast.444), channel_id=1, source_target_pairs={{0,8},{8,16},{16,24},{1,9},{9,17},{17,25},{2,10},{10,18},{18,26},{... | collective-permute-start | bytes 98312 | tf_op jit(solution)/shard_map/ppermute | solution.py:31
  3.0 14.7 %collective-permute-start.3 = (bf16[64,256]{0,1:T(8,128)(2,1)S(1)}, bf16[64,256]{0,1:T(8,128)(2,1)S(1)}, u32[]{:S(2)}, u32[]{:S(2)}) collective-permute-start(bf16[64,256]{0,1:T(8,128)(2,1)S(1)} %bitcast.445), channel_id=1, source_target_pairs={{8,0},{16,8},{24,16},{9,1},{17,9},{25,17},{10,2},{18,10},{26,18},{... | collective-permute-start | bytes 98312 | tf_op jit(solution)/shard_map/ppermute | solution.py:31
  7.3 8.6 %collective-permute-start = (bf16[64,1,128]{0,2,1:T(8,128)(2,1)}, bf16[64,1,128]{0,2,1:T(8,128)(2,1)}, u32[]{:S(2)}, u32[]{:S(2)}) collective-permute-start(bf16[64,1,128]{0,2,1:T(8,128)(2,1)} %get-tuple-element.20), channel_id=1, source_target_pairs={{0,1},{1,2},{2,3},{3,4},{4,5},{5,6},{6,7},{7,0},{8,9},{9,10},{10,1... | collective-permute-start | bytes 49160 | tf_op jit(solution)/shard_map/ppermute | solution.py:22
  7.5 9.2 %collective-permute-start.1 = (bf16[64,1,128]{0,2,1:T(8,128)(2,1)}, bf16[64,1,128]{0,2,1:T(8,128)(2,1)}, u32[]{:S(2)}, u32[]{:S(2)}) collective-permute-start(bf16[64,1,128]{0,2,1:T(8,128)(2,1)} %get-tuple-element.19), channel_id=1, source_target_pairs={{1,0},{2,1},{3,2},{4,3},{5,4},{6,5},{7,6},{0,7},{9,8},{10,9},{11,1... | collective-permute-start | bytes 49160 | tf_op jit(solution)/shard_map/ppermute | solution.py:23
  11.8 7.8 %copy-start.4 = (s32[1024]{0:T(1024)}, s32[1024]{0:T(1024)S(1)}, u32[]{:S(2)}) copy-start(s32[1024]{0:T(1024)S(1)} %get-tuple-element.51) | copy-start | bytes 12292
  13.6 7.4 %copy-start.1 = (bf16[1,1,16,128,128]{4,3,2,1,0:T(8,128)(2,1)S(1)}, bf16[1,1,16,128,128]{4,3,2,1,0:T(8,128)(2,1)}, u32[]{:S(2)}) copy-start(bf16[1,1,16,128,128]{4,3,2,1,0:T(8,128)(2,1)} %param.27) | copy-start | bytes 1572868
  18.0 0.7 copy-start.2
  19.7 4.2 %copy-start.5 = (pred[16,128]{1,0:T(8,128)(4,1)S(1)}, pred[16,128]{1,0:T(8,128)(4,1)}, u32[]{:S(2)}) copy-start(pred[16,128]{1,0:T(8,128)(4,1)} %fusion.161) | copy-start | bytes 6148
  26.1 16.8 %collective-permute-start.6 = (bf16[64,256]{1,0:T(8,128)(2,1)S(1)}, bf16[64,256]{1,0:T(8,128)(2,1)S(1)}, u32[]{:S(2)}, u32[]{:S(2)}) collective-permute-start(bf16[64,256]{1,0:T(8,128)(2,1)S(1)} %get-tuple-element.18), channel_id=1, source_target_pairs={{0,8},{8,16},{16,24},{1,9},{9,17},{17,25},{2,10},{10,18},{18,26},{... | collective-permute-start | bytes 98312 | tf_op jit(solution)/shard_map/ppermute | solution.py:31
  28.0 15.3 %collective-permute-start.7 = (bf16[64,256]{1,0:T(8,128)(2,1)S(1)}, bf16[64,256]{1,0:T(8,128)(2,1)S(1)}, u32[]{:S(2)}, u32[]{:S(2)}) collective-permute-start(bf16[64,256]{1,0:T(8,128)(2,1)S(1)} %get-tuple-element.18), channel_id=1, source_target_pairs={{8,0},{16,8},{24,16},{9,1},{17,9},{25,17},{10,2},{18,10},{26,18},{... | collective-permute-start | bytes 98312 | tf_op jit(solution)/shard_map/ppermute | solution.py:31
  31.8 4.7 %collective-permute-start.4 = (bf16[64,1,128]{2,0,1:T(8,128)(2,1)S(1)}, bf16[64,1,128]{2,0,1:T(8,128)(2,1)S(1)}, u32[]{:S(2)}, u32[]{:S(2)}) collective-permute-start(bf16[64,1,128]{2,0,1:T(8,128)(2,1)S(1)} %copy.254), channel_id=1, source_target_pairs={{0,1},{1,2},{2,3},{3,4},{4,5},{5,6},{6,7},{7,0},{8,9},{9,10},{10,1... | collective-permute-start | bytes 49160 | tf_op jit(solution)/shard_map/ppermute | solution.py:22
  36.4 6.5 %collective-permute-start.5 = (bf16[64,1,128]{2,0,1:T(8,128)(2,1)S(1)}, bf16[64,1,128]{2,0,1:T(8,128)(2,1)S(1)}, u32[]{:S(2)}, u32[]{:S(2)}) collective-permute-start(bf16[64,1,128]{2,0,1:T(8,128)(2,1)S(1)} %copy.255), channel_id=1, source_target_pairs={{1,0},{2,1},{3,2},{4,3},{5,4},{6,5},{7,6},{0,7},{9,8},{10,9},{11,1... | collective-permute-start | bytes 49160 | tf_op jit(solution)/shard_map/ppermute | solution.py:23
  42.9 0.9 copy-start.3
  53.1 14.6 %collective-permute-start.10 = (bf16[64,256]{1,0:T(8,128)(2,1)S(1)}, bf16[64,256]{1,0:T(8,128)(2,1)S(1)}, u32[]{:S(2)}, u32[]{:S(2)}) collective-permute-start(bf16[64,256]{1,0:T(8,128)(2,1)S(1)} %get-tuple-element.16), channel_id=1, source_target_pairs={{0,8},{8,16},{16,24},{1,9},{9,17},{17,25},{2,10},{10,18},{18,26},{... | collective-permute-start | bytes 98312 | tf_op jit(solution)/shard_map/ppermute | solution.py:31
  55.0 13.1 %collective-permute-start.11 = (bf16[64,256]{1,0:T(8,128)(2,1)S(1)}, bf16[64,256]{1,0:T(8,128)(2,1)S(1)}, u32[]{:S(2)}, u32[]{:S(2)}) collective-permute-start(bf16[64,256]{1,0:T(8,128)(2,1)S(1)} %get-tuple-element.16), channel_id=1, source_target_pairs={{8,0},{16,8},{24,16},{9,1},{17,9},{25,17},{10,2},{18,10},{26,18},{... | collective-permute-start | bytes 98312 | tf_op jit(solution)/shard_map/ppermute | solution.py:31
  58.7 3.9 %collective-permute-start.8 = (bf16[64,1,128]{2,0,1:T(8,128)(2,1)S(1)}, bf16[64,1,128]{2,0,1:T(8,128)(2,1)S(1)}, u32[]{:S(2)}, u32[]{:S(2)}) collective-permute-start(bf16[64,1,128]{2,0,1:T(8,128)(2,1)S(1)} %copy.256), channel_id=1, source_target_pairs={{0,1},{1,2},{2,3},{3,4},{4,5},{5,6},{6,7},{7,0},{8,9},{9,10},{10,1... | collective-permute-start | bytes 49160 | tf_op jit(solution)/shard_map/ppermute | solution.py:22
  60.5 6.5 %collective-permute-start.9 = (bf16[64,1,128]{2,0,1:T(8,128)(2,1)S(1)}, bf16[64,1,128]{2,0,1:T(8,128)(2,1)S(1)}, u32[]{:S(2)}, u32[]{:S(2)}) collective-permute-start(bf16[64,1,128]{2,0,1:T(8,128)(2,1)S(1)} %copy.257), channel_id=1, source_target_pairs={{1,0},{2,1},{3,2},{4,3},{5,4},{6,5},{7,6},{0,7},{9,8},{10,9},{11,1... | collective-permute-start | bytes 49160 | tf_op jit(solution)/shard_map/ppermute | solution.py:23
  77.8 14.5 %collective-permute-start.14 = (bf16[64,256]{1,0:T(8,128)(2,1)S(1)}, bf16[64,256]{1,0:T(8,128)(2,1)S(1)}, u32[]{:S(2)}, u32[]{:S(2)}) collective-permute-start(bf16[64,256]{1,0:T(8,128)(2,1)S(1)} %get-tuple-element.14), channel_id=1, source_target_pairs={{0,8},{8,16},{16,24},{1,9},{9,17},{17,25},{2,10},{10,18},{18,26},{... | collective-permute-start | bytes 98312 | tf_op jit(solution)/shard_map/ppermute | solution.py:31
  79.7 13.1 %collective-permute-start.15 = (bf16[64,256]{1,0:T(8,128)(2,1)S(1)}, bf16[64,256]{1,0:T(8,128)(2,1)S(1)}, u32[]{:S(2)}, u32[]{:S(2)}) collective-permute-start(bf16[64,256]{1,0:T(8,128)(2,1)S(1)} %get-tuple-element.14), channel_id=1, source_target_pairs={{8,0},{16,8},{24,16},{9,1},{17,9},{25,17},{10,2},{18,10},{26,18},{... | collective-permute-start | bytes 98312 | tf_op jit(solution)/shard_map/ppermute | solution.py:31
  83.4 3.9 %collective-permute-start.12 = (bf16[64,1,128]{2,0,1:T(8,128)(2,1)S(1)}, bf16[64,1,128]{2,0,1:T(8,128)(2,1)S(1)}, u32[]{:S(2)}, u32[]{:S(2)}) collective-permute-start(bf16[64,1,128]{2,0,1:T(8,128)(2,1)S(1)} %copy.258), channel_id=1, source_target_pairs={{0,1},{1,2},{2,3},{3,4},{4,5},{5,6},{6,7},{7,0},{8,9},{9,10},{10,1... | collective-permute-start | bytes 49160 | tf_op jit(solution)/shard_map/ppermute | solution.py:22
  85.2 6.5 %collective-permute-start.13 = (bf16[64,1,128]{2,0,1:T(8,128)(2,1)S(1)}, bf16[64,1,128]{2,0,1:T(8,128)(2,1)S(1)}, u32[]{:S(2)}, u32[]{:S(2)}) collective-permute-start(bf16[64,1,128]{2,0,1:T(8,128)(2,1)S(1)} %copy.259), channel_id=1, source_target_pairs={{1,0},{2,1},{3,2},{4,3},{5,4},{6,5},{7,6},{0,7},{9,8},{10,9},{11,1... | collective-permute-start | bytes 49160 | tf_op jit(solution)/shard_map/ppermute | solution.py:23
  102.5 14.6 %collective-permute-start.18 = (bf16[64,256]{1,0:T(8,128)(2,1)S(1)}, bf16[64,256]{1,0:T(8,128)(2,1)S(1)}, u32[]{:S(2)}, u32[]{:S(2)}) collective-permute-start(bf16[64,256]{1,0:T(8,128)(2,1)S(1)} %get-tuple-element.12), channel_id=1, source_target_pairs={{0,8},{8,16},{16,24},{1,9},{9,17},{17,25},{2,10},{10,18},{18,26},{... | collective-permute-start | bytes 98312 | tf_op jit(solution)/shard_map/ppermute | solution.py:31
  104.4 13.1 %collective-permute-start.19 = (bf16[64,256]{1,0:T(8,128)(2,1)S(1)}, bf16[64,256]{1,0:T(8,128)(2,1)S(1)}, u32[]{:S(2)}, u32[]{:S(2)}) collective-permute-start(bf16[64,256]{1,0:T(8,128)(2,1)S(1)} %get-tuple-element.12), channel_id=1, source_target_pairs={{8,0},{16,8},{24,16},{9,1},{17,9},{25,17},{10,2},{18,10},{26,18},{... | collective-permute-start | bytes 98312 | tf_op jit(solution)/shard_map/ppermute | solution.py:31
  108.1 3.9 %collective-permute-start.16 = (bf16[64,1,128]{2,0,1:T(8,128)(2,1)S(1)}, bf16[64,1,128]{2,0,1:T(8,128)(2,1)S(1)}, u32[]{:S(2)}, u32[]{:S(2)}) collective-permute-start(bf16[64,1,128]{2,0,1:T(8,128)(2,1)S(1)} %copy.260), channel_id=1, source_target_pairs={{0,1},{1,2},{2,3},{3,4},{4,5},{5,6},{6,7},{7,0},{8,9},{9,10},{10,1... | collective-permute-start | bytes 49160 | tf_op jit(solution)/shard_map/ppermute | solution.py:22
  110.0 6.5 %collective-permute-start.17 = (bf16[64,1,128]{2,0,1:T(8,128)(2,1)S(1)}, bf16[64,1,128]{2,0,1:T(8,128)(2,1)S(1)}, u32[]{:S(2)}, u32[]{:S(2)}) collective-permute-start(bf16[64,1,128]{2,0,1:T(8,128)(2,1)S(1)} %copy.261), channel_id=1, source_target_pairs={{1,0},{2,1},{3,2},{4,3},{5,4},{6,5},{7,6},{0,7},{9,8},{10,9},{11,1... | collective-permute-start | bytes 49160 | tf_op jit(solution)/shard_map/ppermute | solution.py:23
  127.2 14.6 %collective-permute-start.22 = (bf16[64,256]{1,0:T(8,128)(2,1)S(1)}, bf16[64,256]{1,0:T(8,128)(2,1)S(1)}, u32[]{:S(2)}, u32[]{:S(2)}) collective-permute-start(bf16[64,256]{1,0:T(8,128)(2,1)S(1)} %get-tuple-element.10), channel_id=1, source_target_pairs={{0,8},{8,16},{16,24},{1,9},{9,17},{17,25},{2,10},{10,18},{18,26},{... | collective-permute-start | bytes 98312 | tf_op jit(solution)/shard_map/ppermute | solution.py:31
  129.1 13.1 %collective-permute-start.23 = (bf16[64,256]{1,0:T(8,128)(2,1)S(1)}, bf16[64,256]{1,0:T(8,128)(2,1)S(1)}, u32[]{:S(2)}, u32[]{:S(2)}) collective-permute-start(bf16[64,256]{1,0:T(8,128)(2,1)S(1)} %get-tuple-element.10), channel_id=1, source_target_pairs={{8,0},{16,8},{24,16},{9,1},{17,9},{25,17},{10,2},{18,10},{26,18},{... | collective-permute-start | bytes 98312 | tf_op jit(solution)/shard_map/ppermute | solution.py:31
  132.9 3.9 %collective-permute-start.20 = (bf16[64,1,128]{2,0,1:T(8,128)(2,1)S(1)}, bf16[64,1,128]{2,0,1:T(8,128)(2,1)S(1)}, u32[]{:S(2)}, u32[]{:S(2)}) collective-permute-start(bf16[64,1,128]{2,0,1:T(8,128)(2,1)S(1)} %copy.262), channel_id=1, source_target_pairs={{0,1},{1,2},{2,3},{3,4},{4,5},{5,6},{6,7},{7,0},{8,9},{9,10},{10,1... | collective-permute-start | bytes 49160 | tf_op jit(solution)/shard_map/ppermute | solution.py:22
  134.7 6.5 %collective-permute-start.21 = (bf16[64,1,128]{2,0,1:T(8,128)(2,1)S(1)}, bf16[64,1,128]{2,0,1:T(8,128)(2,1)S(1)}, u32[]{:S(2)}, u32[]{:S(2)}) collective-permute-start(bf16[64,1,128]{2,0,1:T(8,128)(2,1)S(1)} %copy.263), channel_id=1, source_target_pairs={{1,0},{2,1},{3,2},{4,3},{5,4},{6,5},{7,6},{0,7},{9,8},{10,9},{11,1... | collective-permute-start | bytes 49160 | tf_op jit(solution)/shard_map/ppermute | solution.py:23
  151.9 14.7 %collective-permute-start.26 = (bf16[64,256]{1,0:T(8,128)(2,1)S(1)}, bf16[64,256]{1,0:T(8,128)(2,1)S(1)}, u32[]{:S(2)}, u32[]{:S(2)}) collective-permute-start(bf16[64,256]{1,0:T(8,128)(2,1)S(1)} %get-tuple-element.8), channel_id=1, source_target_pairs={{0,8},{8,16},{16,24},{1,9},{9,17},{17,25},{2,10},{10,18},{18,26},{... | collective-permute-start | bytes 98312 | tf_op jit(solution)/shard_map/ppermute | solution.py:31
  153.8 13.2 %collective-permute-start.27 = (bf16[64,256]{1,0:T(8,128)(2,1)S(1)}, bf16[64,256]{1,0:T(8,128)(2,1)S(1)}, u32[]{:S(2)}, u32[]{:S(2)}) collective-permute-start(bf16[64,256]{1,0:T(8,128)(2,1)S(1)} %get-tuple-element.8), channel_id=1, source_target_pairs={{8,0},{16,8},{24,16},{9,1},{17,9},{25,17},{10,2},{18,10},{26,18},{... | collective-permute-start | bytes 98312 | tf_op jit(solution)/shard_map/ppermute | solution.py:31
  157.6 4.1 %collective-permute-start.24 = (bf16[64,1,128]{2,0,1:T(8,128)(2,1)S(1)}, bf16[64,1,128]{2,0,1:T(8,128)(2,1)S(1)}, u32[]{:S(2)}, u32[]{:S(2)}) collective-permute-start(bf16[64,1,128]{2,0,1:T(8,128)(2,1)S(1)} %copy.264), channel_id=1, source_target_pairs={{0,1},{1,2},{2,3},{3,4},{4,5},{5,6},{6,7},{7,0},{8,9},{9,10},{10,1... | collective-permute-start | bytes 49160 | tf_op jit(solution)/shard_map/ppermute | solution.py:22
  159.5 6.5 %collective-permute-start.25 = (bf16[64,1,128]{2,0,1:T(8,128)(2,1)S(1)}, bf16[64,1,128]{2,0,1:T(8,128)(2,1)S(1)}, u32[]{:S(2)}, u32[]{:S(2)}) collective-permute-start(bf16[64,1,128]{2,0,1:T(8,128)(2,1)S(1)} %copy.265), channel_id=1, source_target_pairs={{1,0},{2,1},{3,2},{4,3},{5,4},{6,5},{7,6},{0,7},{9,8},{10,9},{11,1... | collective-permute-start | bytes 49160 | tf_op jit(solution)/shard_map/ppermute | solution.py:23
  176.8 14.6 %collective-permute-start.30 = (bf16[64,256]{1,0:T(8,128)(2,1)S(1)}, bf16[64,256]{1,0:T(8,128)(2,1)S(1)}, u32[]{:S(2)}, u32[]{:S(2)}) collective-permute-start(bf16[64,256]{1,0:T(8,128)(2,1)S(1)} %get-tuple-element.6), channel_id=1, source_target_pairs={{0,8},{8,16},{16,24},{1,9},{9,17},{17,25},{2,10},{10,18},{18,26},{... | collective-permute-start | bytes 98312 | tf_op jit(solution)/shard_map/ppermute | solution.py:31
  178.7 13.1 %collective-permute-start.31 = (bf16[64,256]{1,0:T(8,128)(2,1)S(1)}, bf16[64,256]{1,0:T(8,128)(2,1)S(1)}, u32[]{:S(2)}, u32[]{:S(2)}) collective-permute-start(bf16[64,256]{1,0:T(8,128)(2,1)S(1)} %get-tuple-element.6), channel_id=1, source_target_pairs={{8,0},{16,8},{24,16},{9,1},{17,9},{25,17},{10,2},{18,10},{26,18},{... | collective-permute-start | bytes 98312 | tf_op jit(solution)/shard_map/ppermute | solution.py:31
  182.4 3.9 %collective-permute-start.28 = (bf16[64,1,128]{2,0,1:T(8,128)(2,1)S(1)}, bf16[64,1,128]{2,0,1:T(8,128)(2,1)S(1)}, u32[]{:S(2)}, u32[]{:S(2)}) collective-permute-start(bf16[64,1,128]{2,0,1:T(8,128)(2,1)S(1)} %copy.266), channel_id=1, source_target_pairs={{0,1},{1,2},{2,3},{3,4},{4,5},{5,6},{6,7},{7,0},{8,9},{9,10},{10,1... | collective-permute-start | bytes 49160 | tf_op jit(solution)/shard_map/ppermute | solution.py:22
  184.3 6.5 %collective-permute-start.29 = (bf16[64,1,128]{2,0,1:T(8,128)(2,1)S(1)}, bf16[64,1,128]{2,0,1:T(8,128)(2,1)S(1)}, u32[]{:S(2)}, u32[]{:S(2)}) collective-permute-start(bf16[64,1,128]{2,0,1:T(8,128)(2,1)S(1)} %copy.267), channel_id=1, source_target_pairs={{1,0},{2,1},{3,2},{4,3},{5,4},{6,5},{7,6},{0,7},{9,8},{10,9},{11,1... | collective-permute-start | bytes 49160 | tf_op jit(solution)/shard_map/ppermute | solution.py:23
where the time goes:
time: 199 us; the launch traced here: 198 us
  starting transfers between devices  62.4 us (31%)
  local copies, waits for them, and re-layouts  60.2 us (30%)
  matrix products  43.3 us (22%)
  waiting for transfers between devices  29.4 us (15%)
    ppermute x16, starting transfers between devices, shifted(): return lax.ppermute(value, axis, pairs)  44.5 us
    ppermute x8, waiting for transfers between devices, with_halo(): after = lax.ppermute(initial, axis, down)  29.3 us
    unnamed x60, local copies, waits for them, and re-layouts  19.6 us
    dot_general x8, matrix products, per_device(): current = jnp.dot(features, read_weight, preferred_element_type=jnp.float32)  17.2 us
    ppermute x8, starting transfers between devices, with_halo(): after = lax.ppermute(initial, axis, down)  14.3 us
    dot_general x8, matrix products, per_device(): jnp.einsum('mbki,bkio->mbo', blocks[:, linked], block_weight, preferred_e...  13.8 us
    gather x8, local copies, waits for them, and re-layouts, per_device(): blocks[:, linked]  13.6 us
    gather x8, local copies, waits for them, and re-layouts, per_device(): chosen = inputs.reshape(members, in_blocks, breadth)[:, block_index]  10.5 us
  transfers between devices with their start and end apart: 32, of which 7 were waited for; matrix products, arithmetic and copies ran while one was open for 16% of the time, Pallas kernels for 0%

commit v1 on v0

v1 whole, which is shorter than its diff:
```python
import functools

import jax
import jax.numpy as jnp
from jax import lax
from jax.experimental import pallas as pl
from jax.experimental.pallas import tpu as pltpu
from jax.sharding import PartitionSpec as P

VARS = 32
OV = 4
STEPS = 8
BLOCK = 128
MESH = pl.DeviceIdType.MESH


def kernel(
    n_lat,
    n_lon,
    lists,
    state,
    reservoir,
    coupling,
    entry,
    read,
    out,
    u0,
    r,
    cw,
    iw,
    rw,
    nsw,
    acc,
    send,
    we_in,
    ns_in,
    outbuf,
    send_sem,
    recv_sem,
    load_sem,
    out_sem,
):
    members = u0.shape[0]
    blocks = cw.shape[0]
    links = cw.shape[1] // BLOCK
    pairs = blocks // 2
    own_pairs = [m for m in range(pairs) if m % 3 == 0]
    we_pairs = [m for m in range(pairs) if m % 3 == 1]
    ns_pairs = [m for m in range(pairs) if m % 3 == 2]

    band = lax.axis_index("lat")
    sector = lax.axis_index("lon")
    east = (band, lax.rem(sector + 1, n_lon))
    west = (band, lax.rem(sector + n_lon - 1, n_lon))
    south = (lax.rem(band + 1, n_lat), sector)
    north = (lax.rem(band + n_lat - 1, n_lat), sector)
    has_north = band > 0
    has_south = band < n_lat - 1

    loads = [
        pltpu.make_async_copy(src, dst, load_sem.at[i])
        for i, (src, dst) in enumerate(
            [(state, u0), (reservoir, r), (coupling, cw), (entry, iw), (read, rw)]
        )
    ]
    for load in loads:
        load.start()

    barrier = pltpu.get_barrier_semaphore()
    pl.semaphore_signal(barrier, inc=1, device_id=east, device_id_type=MESH)
    pl.semaphore_signal(barrier, inc=1, device_id=west, device_id_type=MESH)

    @pl.when(has_south)
    def _():
        pl.semaphore_signal(barrier, inc=1, device_id=south, device_id_type=MESH)

    @pl.when(has_north)
    def _():
        pl.semaphore_signal(barrier, inc=1, device_id=north, device_id_type=MESH)

    def remote(t, src, dst, side, target):
        return pltpu.make_async_remote_copy(
            src_ref=src,
            dst_ref=dst,
            send_sem=send_sem.at[t, side],
            recv_sem=recv_sem.at[t, side],
            device_id=target,
            device_id_type=MESH,
        )

    def to_east(t):
        return remote(t, send.at[t, 1], we_in.at[t, 0], 0, east)

    def to_west(t):
        return remote(t, send.at[t, 0], we_in.at[t, 1], 1, west)

    def to_south(t):
        return remote(t, send.at[t], ns_in.at[t, 0], 2, south)

    def to_north(t):
        return remote(t, send.at[t], ns_in.at[t, 1], 3, north)

    def start_sends(t):
        to_east(t).start()
        to_west(t).start()

        @pl.when(has_south)
        def _():
            to_south(t).start()

        @pl.when(has_north)
        def _():
            to_north(t).start()

    def wait_sends(t):
        to_east(t).wait_send()
        to_west(t).wait_send()

        @pl.when(has_south)
        def _():
            to_south(t).wait_send()

        @pl.when(has_north)
        def _():
            to_north(t).wait_send()

    def put_state(t, value):
        rounded = value.astype(jnp.bfloat16)
        send[t, 0] = rounded[:, :BLOCK]
        send[t, 1] = rounded[:, BLOCK:]

    def dot(a, b):
        return jnp.dot(a, b, preferred_element_type=jnp.float32)

    loads[0].wait()
    put_state(0, u0[...])
    pl.semaphore_wait(
        barrier, 2 + has_north.astype(jnp.int32) + has_south.astype(jnp.int32)
    )
    start_sends(0)

    @pl.when(jnp.logical_not(has_north))
    def _():
        for t in range(STEPS):
            ns_in[t, 0] = jnp.zeros(ns_in.shape[2:], ns_in.dtype)

    @pl.when(jnp.logical_not(has_south))
    def _():
        for t in range(STEPS):
            ns_in[t, 1] = jnp.zeros(ns_in.shape[2:], ns_in.dtype)

    row = lax.broadcasted_iota(jnp.int32, (2 * BLOCK, BLOCK), 0)
    col = lax.broadcasted_iota(jnp.int32, (2 * BLOCK, BLOCK), 1)
    loads[3].wait()
    for side in range(2):
        target = jnp.full((2 * BLOCK, BLOCK), -VARS, jnp.int32)
        for s in range(OV):
            here = (col >= s * VARS) & (col < (s + 1) * VARS)
            target = jnp.where(here, lists[side, s] * VARS + (col - s * VARS), target)
        onehot = jnp.where(row == target, 1.0, 0.0).astype(jnp.bfloat16)
        for n, m in enumerate(ns_pairs):
            nsw[2 * n + side] = dot(onehot, iw[2 * m + side]).astype(jnp.bfloat16)

    for i in (1, 2, 4):
        loads[i].wait()

    even = lax.broadcasted_iota(jnp.int32, (members, 2 * BLOCK), 1) % 2 == 0

    def couple(b):
        first = min(links, blocks - b)
        total = dot(r[:, b * BLOCK : (b + first) * BLOCK], cw[b, : first * BLOCK])
        if first < links:
            total += dot(r[:, : (links - first) * BLOCK], cw[b, first * BLOCK :])
        return total

    def finish(m, activation):
        held = slice(2 * m * BLOCK, 2 * (m + 1) * BLOCK)
        fresh = jnp.tanh(activation).astype(jnp.bfloat16)
        r[:, held] = fresh
        wide = fresh.astype(jnp.float32)
        features = jnp.where(even, wide * wide, wide).astype(jnp.bfloat16)
        return dot(features, rw[held, :])

    @pl.loop(0, STEPS)
    def _(t):
        own = [send[t, c] for c in range(2)]
        for m in own_pairs + ns_pairs + we_pairs:
            for c in range(2):
                b = 2 * m + c
                total = couple(b)
                if m in own_pairs:
                    total += dot(own[c], iw[b])
                acc[:, b * BLOCK : (b + 1) * BLOCK] = total

        def pair_acc(m):
            return acc[:, 2 * m * BLOCK : 2 * (m + 1) * BLOCK]

        result = sum(finish(m, pair_acc(m)) for m in own_pairs)

        @pl.when(t > 0)
        def _():
            wait_sends(t - 1)
            pltpu.make_async_copy(
                outbuf.at[t - 1], out.at[t - 1], out_sem.at[t - 1]
            ).wait()

        @pl.when(has_north)
        def _():
            to_south(t).wait_recv()

        @pl.when(has_south)
        def _():
            to_north(t).wait_recv()

        sides = [
            jnp.concatenate([ns_in[t, side, 0], ns_in[t, side, 1]], axis=1)
            for side in range(2)
        ]
        for n, m in enumerate(ns_pairs):
            entered = [dot(sides[side], nsw[2 * n + side]) for side in range(2)]
            result += finish(m, pair_acc(m) + jnp.concatenate(entered, axis=1))

        to_east(t).wait_recv()
        to_west(t).wait_recv()
        for m in we_pairs:
            entered = [dot(we_in[t, side], iw[2 * m + side]) for side in range(2)]
            result += finish(m, pair_acc(m) + jnp.concatenate(entered, axis=1))

        @pl.when(t < STEPS - 1)
        def _():
            put_state(t + 1, result)
            start_sends(t + 1)

        outbuf[t] = result
        pltpu.make_async_copy(outbuf.at[t], out.at[t], out_sem.at[t]).start()

    last = STEPS - 1
    wait_sends(last)
    pltpu.make_async_copy(outbuf.at[last], out.at[last], out_sem.at[last]).wait()


def per_device(n_lat, n_lon, initial_state, initial_reservoir, coupling, input_weight, readout, intersection):
    state = initial_state[0, 0]
    reservoir = initial_reservoir[0, 0]
    entry = input_weight[0, 0]
    read = readout[0, 0]
    lists = intersection[0, 0]
    members, features = state.shape
    nodes = reservoir.shape[1]
    blocks, links = coupling.shape[2], coupling.shape[3]
    weights = coupling[0, 0].reshape(blocks, links * BLOCK, BLOCK)
    ns_count = 2 * len([m for m in range(blocks // 2) if m % 3 == 2])
    hbm = pl.BlockSpec(memory_space=pltpu.MemorySpace.HBM)
    bf16, f32 = jnp.bfloat16, jnp.float32
    forecast = pl.pallas_call(
        functools.partial(kernel, n_lat, n_lon),
        out_shape=jax.ShapeDtypeStruct((STEPS, members, features), f32),
        in_specs=[pl.BlockSpec(memory_space=pltpu.MemorySpace.SMEM)] + [hbm] * 5,
        out_specs=hbm,
        scratch_shapes=[
            pltpu.VMEM((members, features), f32),
            pltpu.VMEM((members, nodes), bf16),
            pltpu.VMEM((blocks, links * BLOCK, BLOCK), bf16),
            pltpu.VMEM((blocks, BLOCK, BLOCK), bf16),
            pltpu.VMEM((nodes, features), bf16),
            pltpu.VMEM((ns_count, 2 * BLOCK, BLOCK), bf16),
            pltpu.VMEM((members, nodes), f32),
            pltpu.VMEM((STEPS, 2, members, BLOCK), bf16),
            pltpu.VMEM((STEPS, 2, members, BLOCK), bf16),
            pltpu.VMEM((STEPS, 2, 2, members, BLOCK), bf16),
            pltpu.VMEM((STEPS, members, features), f32),
            pltpu.SemaphoreType.DMA((STEPS, 4)),
            pltpu.SemaphoreType.DMA((STEPS, 4)),
            pltpu.SemaphoreType.DMA((5,)),
            pltpu.SemaphoreType.DMA((STEPS,)),
        ],
        compiler_params=pltpu.CompilerParams(
            collective_id=0, has_side_effects=True, vmem_limit_bytes=24 * 1024 * 1024
        ),
    )(lists, state, reservoir, weights, entry, read)
    return forecast[:, None, None]


def solution(mesh):
    in_specs = (
        P("lat", "lon", None, None),
        P("lat", "lon", None, None),
        P("lat", "lon", None, None, None, None),
        P("lat", "lon", None, None, None),
        P("lat", "lon", None, None),
        P("lat", "lon", None, None),
    )
    out_specs = P(None, "lat", "lon", None, None)
    run = functools.partial(per_device, mesh.shape["lat"], mesh.shape["lon"])
    return jax.shard_map(
        run, mesh=mesh, in_specs=in_specs, out_specs=out_specs, check_vma=False
    )
```

time: 199 us -> 50.7 us (0.25)
  the two profiles are of different devices: /device:TPU:30 before, /device:TPU:0 now
where the time goes in v1:
time: 50.7 us; the launch traced here: 50.4 us
  Pallas kernels  43.3 us (85%)
  local copies, waits for them, and re-layouts  7.12 us (14%)
    pallas_call x1, Pallas kernels, per_device(): pl.pallas_call(functools.partial(kernel, n_lat, n_lon), out_shape=jax.Sha...  43.3 us
    unnamed x13, local copies, waits for them, and re-layouts  7.12 us

profile of v1, /device:TPU:0, one launch (start us, length us, event | category | flops | bytes accessed | tf_op | source)
XLA Modules:
  0.0 50.4 jit_solution(7089312047104253280)
XLA Ops:
  0.0 0.0 copy-start
  0.0 1.6 %copy-done = bf16[1,1,16,4,128,128]{5,4,3,2,1,0:T(8,128)(2,1)S(1)} copy-done((bf16[1,1,16,4,128,128]{5,4,3,2,1,0:T(8,128)(2,1)S(1)}, bf16[1,1,16,4,128,128]{5,4,3,2,1,0:T(8,128)(2,1)}, u32[]{:S(2)}) %copy-start) | copy-done | bytes 2097176
  1.6 0.0 copy-start.1
  1.6 1.2 %copy-done.1 = bf16[1,1,2048,256]{3,2,1,0:T(8,128)(2,1)S(1)} copy-done((bf16[1,1,2048,256]{3,2,1,0:T(8,128)(2,1)S(1)}, bf16[1,1,2048,256]{3,2,1,0:T(8,128)(2,1)}, u32[]{:S(2)}) %copy-start.1) | copy-done | bytes 1048600
  2.8 0.0 copy-start.2
  2.8 1.0 %copy-done.2 = bf16[1,1,16,128,128]{4,3,2,1,0:T(8,128)(2,1)S(1)} copy-done((bf16[1,1,16,128,128]{4,3,2,1,0:T(8,128)(2,1)S(1)}, bf16[1,1,16,128,128]{4,3,2,1,0:T(8,128)(2,1)}, u32[]{:S(2)}) %copy-start.2) | copy-done | bytes 524312
  3.9 0.0 copy-start.3
  3.9 0.9 %copy-done.3 = bf16[1,1,64,2048]{3,2,1,0:T(8,128)(2,1)S(1)} copy-done((bf16[1,1,64,2048]{3,2,1,0:T(8,128)(2,1)S(1)}, bf16[1,1,64,2048]{3,2,1,0:T(8,128)(2,1)}, u32[]{:S(2)}) %copy-start.3) | copy-done | bytes 262168
  4.8 0.0 copy-start.4
  4.8 0.8 %copy-done.4 = f32[1,1,64,256]{3,2,1,0:T(8,128)S(1)} copy-done((f32[1,1,64,256]{3,2,1,0:T(8,128)S(1)}, f32[1,1,64,256]{3,2,1,0:T(8,128)}, u32[]{:S(2)}) %copy-start.4) | copy-done | bytes 65560
  5.7 0.0 copy-start.5
  5.7 0.7 %copy-done.5 = s32[1,1,2,4]{3,2,1,0:T(2,128)S(1)} copy-done((s32[1,1,2,4]{3,2,1,0:T(2,128)S(1)}, s32[1,1,2,4]{3,2,1,0:T(2,128)}, u32[]{:S(2)}) %copy-start.5) | copy-done | bytes 56
  6.3 43.3 %shard_map.64 = f32[8,64,256]{2,1,0:T(8,128)S(1)} custom-call(s32[2,4]{1,0:T(2,128)S(1)} %bitcast.15, f32[64,256]{1,0:T(8,128)S(1)} %bitcast.14, bf16[64,2048]{1,0:T(8,128)(2,1)S(1)} %bitcast.13, bf16[16,512,128]{2,1,0:T(8,128)(2,1)S(1)} %bitcast.9, bf16[16,128,128]{2,1,0:T(8,128)(2,1)S(1)} %bitcast.12, bf16[2048,256]{1,0:T(8,128)(2,1)S(1)} %bitcast.11), custom_call_target="tpu_custom_call" | custom-call | tf_op jit(solution)/shard_map/pallas_call | solution.py:255
  49.6 0.8 %copy.9 = f32[8,1,1,64,256]{4,3,2,1,0:T(8,128)} copy(f32[8,1,1,64,256]{4,3,2,1,0:T(8,128)S(1)} %bitcast.10) | data formatting | bytes 1048576
Async XLA Ops:
  0.0 1.6 %copy-start = (bf16[1,1,16,4,128,128]{5,4,3,2,1,0:T(8,128)(2,1)S(1)}, bf16[1,1,16,4,128,128]{5,4,3,2,1,0:T(8,128)(2,1)}, u32[]{:S(2)}) copy-start(bf16[1,1,16,4,128,128]{5,4,3,2,1,0:T(8,128)(2,1)} %param.8) | copy-start | bytes 6291460
  1.6 1.2 %copy-start.1 = (bf16[1,1,2048,256]{3,2,1,0:T(8,128)(2,1)S(1)}, bf16[1,1,2048,256]{3,2,1,0:T(8,128)(2,1)}, u32[]{:S(2)}) copy-start(bf16[1,1,2048,256]{3,2,1,0:T(8,128)(2,1)} %param.10) | copy-start | bytes 3145732
  2.8 1.0 %copy-start.2 = (bf16[1,1,16,128,128]{4,3,2,1,0:T(8,128)(2,1)S(1)}, bf16[1,1,16,128,128]{4,3,2,1,0:T(8,128)(2,1)}, u32[]{:S(2)}) copy-start(bf16[1,1,16,128,128]{4,3,2,1,0:T(8,128)(2,1)} %param.9) | copy-start | bytes 1572868
  3.9 0.9 %copy-start.3 = (bf16[1,1,64,2048]{3,2,1,0:T(8,128)(2,1)S(1)}, bf16[1,1,64,2048]{3,2,1,0:T(8,128)(2,1)}, u32[]{:S(2)}) copy-start(bf16[1,1,64,2048]{3,2,1,0:T(8,128)(2,1)} %param.7) | copy-start | bytes 786436
  4.8 0.8 %copy-start.4 = (f32[1,1,64,256]{3,2,1,0:T(8,128)S(1)}, f32[1,1,64,256]{3,2,1,0:T(8,128)}, u32[]{:S(2)}) copy-start(f32[1,1,64,256]{3,2,1,0:T(8,128)} %param.6) | copy-start | bytes 196612
  5.7 0.7 %copy-start.5 = (s32[1,1,2,4]{3,2,1,0:T(2,128)S(1)}, s32[1,1,2,4]{3,2,1,0:T(2,128)}, u32[]{:S(2)}) copy-start(s32[1,1,2,4]{3,2,1,0:T(2,128)} %param.11) | copy-start | bytes 100

commit v2 on v1

--- a/solution.py
+++ b/solution.py
@@ -25,6 +25,7 @@
     read,
     out,
     u0,
+    r0,
     r,
     cw,
     iw,
@@ -47,11 +48,15 @@
     own_pairs = [m for m in range(pairs) if m % 3 == 0]
     we_pairs = [m for m in range(pairs) if m % 3 == 1]
     ns_pairs = [m for m in range(pairs) if m % 3 == 2]
+    own_blocks = [2 * m + c for m in own_pairs for c in range(2)]
+    ns_blocks = [2 * m + c for m in ns_pairs for c in range(2)]
 
     band = lax.axis_index("lat")
     sector = lax.axis_index("lon")
     east = (band, lax.rem(sector + 1, n_lon))
     west = (band, lax.rem(sector + n_lon - 1, n_lon))
+    far = lax.rem(sector, 2)
+    near = 1 - far
     south = (lax.rem(band + 1, n_lat), sector)
     north = (lax.rem(band + n_lat - 1, n_lat), sector)
     has_north = band > 0
@@ -60,7 +65,7 @@
     loads = [
         pltpu.make_async_copy(src, dst, load_sem.at[i])
         for i, (src, dst) in enumerate(
-            [(state, u0), (reservoir, r), (coupling, cw), (entry, iw), (read, rw)]
+            [(state, u0), (entry, iw), (reservoir, r0), (coupling, cw), (read, rw)]
         )
     ]
     for load in loads:
@@ -88,11 +93,9 @@
             device_id_type=MESH,
         )
 
-    def to_east(t):
-        return remote(t, send.at[t, 1], we_in.at[t, 0], 0, east)
-
-    def to_west(t):
-        return remote(t, send.at[t, 0], we_in.at[t, 1], 1, west)
+    def to_lon(t, side):
+        target = (band, lax.rem(sector + 2 * side - 1 + n_lon, n_lon))
+        return remote(t, send.at[t, side], we_in.at[t, 1 - side], 1 - side, target)
 
     def to_south(t):
         return remote(t, send.at[t], ns_in.at[t, 0], 2, south)
@@ -101,8 +104,8 @@
         return remote(t, send.at[t], ns_in.at[t, 1], 3, north)
 
     def start_sends(t):
-        to_east(t).start()
-        to_west(t).start()
+        to_lon(t, far).start()
+        to_lon(t, near).start()
 
         @pl.when(has_south)
         def _():
@@ -113,8 +116,8 @@
             to_north(t).start()
 
     def wait_sends(t):
-        to_east(t).wait_send()
-        to_west(t).wait_send()
+        to_lon(t, far).wait_send()
+        to_lon(t, near).wait_send()
 
         @pl.when(has_south)
         def _():
@@ -151,7 +154,7 @@
 
     row = lax.broadcasted_iota(jnp.int32, (2 * BLOCK, BLOCK), 0)
     col = lax.broadcasted_iota(jnp.int32, (2 * BLOCK, BLOCK), 1)
-    loads[3].wait()
+    loads[1].wait()
     for side in range(2):
         target = jnp.full((2 * BLOCK, BLOCK), -VARS, jnp.int32)
         for s in range(OV):
@@ -161,41 +164,40 @@
         for n, m in enumerate(ns_pairs):
             nsw[2 * n + side] = dot(onehot, iw[2 * m + side]).astype(jnp.bfloat16)
 
-    for i in (1, 2, 4):
-        loads[i].wait()
-
-    even = lax.broadcasted_iota(jnp.int32, (members, 2 * BLOCK), 1) % 2 == 0
+    loads[2].wait()
+    for b in range(blocks):
+        r[b] = r0[:, b * BLOCK : (b + 1) * BLOCK]
+    loads[3].wait()
+    loads[4].wait()
+
+    even = lax.broadcasted_iota(jnp.int32, (members, BLOCK), 1) % 2 == 0
 
     def couple(b):
-        first = min(links, blocks - b)
-        total = dot(r[:, b * BLOCK : (b + first) * BLOCK], cw[b, : first * BLOCK])
-        if first < links:
-            total += dot(r[:, : (links - first) * BLOCK], cw[b, first * BLOCK :])
-        return total
-
-    def finish(m, activation):
-        held = slice(2 * m * BLOCK, 2 * (m + 1) * BLOCK)
-        fresh = jnp.tanh(activation).astype(jnp.bfloat16)
-        r[:, held] = fresh
-        wide = fresh.astype(jnp.float32)
-        features = jnp.where(even, wide * wide, wide).astype(jnp.bfloat16)
-        return dot(features, rw[held, :])
+        linked = [r[(b + k) % blocks] for k in range(links)]
+        return dot(jnp.concatenate(linked, axis=1), cw[b])
+
+    def finish(indices, activations):
+        features = []
+        for b, activation in zip(indices, activations):
+            fresh = jnp.tanh(activation).astype(jnp.bfloat16)
+            r[b] = fresh
+            wide = fresh.astype(jnp.float32)
+            features.append(jnp.where(even, wide * wide, wide).astype(jnp.bfloat16))
+        return dot(
+            jnp.concatenate(features, axis=1),
+            jnp.concatenate([rw[b] for b in indices], axis=0),
+        )
 
     @pl.loop(0, STEPS)
     def _(t):
         own = [send[t, c] for c in range(2)]
-        for m in own_pairs + ns_pairs + we_pairs:
-            for c in range(2):
-                b = 2 * m + c
-                total = couple(b)
-                if m in own_pairs:
-                    total += dot(own[c], iw[b])
-                acc[:, b * BLOCK : (b + 1) * BLOCK] = total
-
-        def pair_acc(m):
-            return acc[:, 2 * m * BLOCK : 2 * (m + 1) * BLOCK]
-
-        result = sum(finish(m, pair_acc(m)) for m in own_pairs)
+        for b in range(blocks):
+            total = couple(b)
+            if b in own_blocks:
+                total += dot(own[b % 2], iw[b])
+            acc[b] = total
+
+        result = finish(own_blocks, [acc[b] for b in own_blocks])
 
         @pl.when(t > 0)
         def _():
@@ -216,15 +218,24 @@
             jnp.concatenate([ns_in[t, side, 0], ns_in[t, side, 1]], axis=1)
             for side in range(2)
         ]
-        for n, m in enumerate(ns_pairs):
-            entered = [dot(sides[side], nsw[2 * n + side]) for side in range(2)]
-            result += finish(m, pair_acc(m) + jnp.concatenate(entered, axis=1))
-
-        to_east(t).wait_recv()
-        to_west(t).wait_recv()
-        for m in we_pairs:
-            entered = [dot(we_in[t, side], iw[2 * m + side]) for side in range(2)]
-            result += finish(m, pair_acc(m) + jnp.concatenate(entered, axis=1))
+        result += finish(
+            ns_blocks,
+            [acc[b] + dot(sides[b % 2], nsw[n]) for n, b in enumerate(ns_blocks)],
+        )
+
+        for side in (near, far):
+            to_lon(t, 1 - side).wait_recv()
+            indices = [2 * m + side for m in we_pairs]
+            entered = dot(
+                we_in[t, side], jnp.concatenate([iw[b] for b in indices], axis=1)
+            )
+            result += finish(
+                indices,
+                [
+                    acc[b] + entered[:, n * BLOCK : (n + 1) * BLOCK]
+                    for n, b in enumerate(indices)
+                ],
+            )
 
         @pl.when(t < STEPS - 1)
         def _():
@@ -243,11 +254,11 @@
     state = initial_state[0, 0]
     reservoir = initial_reservoir[0, 0]
     entry = input_weight[0, 0]
-    read = readout[0, 0]
     lists = intersection[0, 0]
     members, features = state.shape
     nodes = reservoir.shape[1]
     blocks, links = coupling.shape[2], coupling.shape[3]
+    read = readout[0, 0].reshape(blocks, BLOCK, features)
     weights = coupling[0, 0].reshape(blocks, links * BLOCK, BLOCK)
     ns_count = 2 * len([m for m in range(blocks // 2) if m % 3 == 2])
     hbm = pl.BlockSpec(memory_space=pltpu.MemorySpace.HBM)
@@ -260,11 +271,12 @@
         scratch_shapes=[
             pltpu.VMEM((members, features), f32),
             pltpu.VMEM((members, nodes), bf16),
+            pltpu.VMEM((blocks, members, BLOCK), bf16),
             pltpu.VMEM((blocks, links * BLOCK, BLOCK), bf16),
             pltpu.VMEM((blocks, BLOCK, BLOCK), bf16),
-            pltpu.VMEM((nodes, features), bf16),
+            pltpu.VMEM((blocks, BLOCK, features), bf16),
             pltpu.VMEM((ns_count, 2 * BLOCK, BLOCK), bf16),
-            pltpu.VMEM((members, nodes), f32),
+            pltpu.VMEM((blocks, members, BLOCK), f32),
             pltpu.VMEM((STEPS, 2, members, BLOCK), bf16),
             pltpu.VMEM((STEPS, 2, members, BLOCK), bf16),
             pltpu.VMEM((STEPS, 2, 2, members, BLOCK), bf16),
@@ -275,7 +287,7 @@
             pltpu.SemaphoreType.DMA((STEPS,)),
         ],
         compiler_params=pltpu.CompilerParams(
-            collective_id=0, has_side_effects=True, vmem_limit_bytes=24 * 1024 * 1024
+            collective_id=0, has_side_effects=True, vmem_limit_bytes=63 * 1024 * 1024
         ),
     )(lists, state, reservoir, weights, entry, read)
     return forecast[:, None, None]

time: 50.7 us -> 45 us (0.89)
  local copies, waits for them, and re-layouts: 7.12 us -> 1.87 us
    unnamed x13 -> x1, local copies, waits for them, and re-layouts: 7.12 us -> 1.87 us
where the time goes in v2:
time: 45 us; the launch traced here: 44.8 us
  Pallas kernels  43 us (96%)
  local copies, waits for them, and re-layouts  1.87 us (4%)
    pallas_call x1, Pallas kernels, per_device(): pl.pallas_call(functools.partial(kernel, n_lat, n_lon), out_shape=jax.Sha...  43 us
    unnamed x1, local copies, waits for them, and re-layouts  1.87 us

profile of v2, /device:TPU:0, one launch (start us, length us, event | category | flops | bytes accessed | tf_op | source)
XLA Modules:
  0.0 44.8 jit_solution(3810899143016436753)
XLA Ops:
  0.0 43.0 %shard_map.64 = f32[8,64,256]{2,1,0:T(8,128)} custom-call(s32[2,4]{1,0:T(2,128)} %bitcast.15, f32[64,256]{1,0:T(8,128)} %bitcast.14, bf16[64,2048]{1,0:T(8,128)(2,1)} %bitcast.13, bf16[16,512,128]{2,1,0:T(8,128)(2,1)} %bitcast.9, bf16[16,128,128]{2,1,0:T(8,128)(2,1)} %bitcast.12, bf16[16,128,256]{2,1,0:T(8,128)(2,1)} %bitcast.11), custom_call_target="tpu_custom_call" | custom-call | tf_op jit(solution)/shard_map/pallas_call | solution.py:266
  43.0 1.9 %copy.9 = f32[8,1,1,64,256]{4,3,2,1,0:T(8,128)} copy(f32[8,1,1,64,256]{4,3,2,1,0:T(8,128)} %bitcast.10) | data formatting | bytes 1048576

commit v3 on v2

--- a/solution.py
+++ b/solution.py
@@ -39,11 +39,13 @@
     send_sem,
     recv_sem,
     load_sem,
+    pair_sem,
     out_sem,
 ):
     members = u0.shape[0]
-    blocks = cw.shape[0]
-    links = cw.shape[1] // BLOCK
+    blocks = coupling.shape[0]
+    depth = coupling.shape[1]
+    links = depth // BLOCK
     pairs = blocks // 2
     own_pairs = [m for m in range(pairs) if m % 3 == 0]
     we_pairs = [m for m in range(pairs) if m % 3 == 1]
@@ -62,26 +64,47 @@
     has_north = band > 0
     has_south = band < n_lat - 1
 
+    barrier = pltpu.get_barrier_semaphore()
+    pl.semaphore_signal(barrier, inc=1, device_id=east, device_id_type=MESH)
+    pl.semaphore_signal(barrier, inc=1, device_id=west, device_id_type=MESH)
+
+    @pl.when(has_south)
+    def _():
+        pl.semaphore_signal(barrier, inc=1, device_id=south, device_id_type=MESH)
+
+    @pl.when(has_north)
+    def _():
+        pl.semaphore_signal(barrier, inc=1, device_id=north, device_id_type=MESH)
+
     loads = [
         pltpu.make_async_copy(src, dst, load_sem.at[i])
         for i, (src, dst) in enumerate(
-            [(state, u0), (entry, iw), (reservoir, r0), (coupling, cw), (read, rw)]
+            [(state, u0), (entry, iw), (reservoir, r0), (read, rw)]
         )
     ]
-    for load in loads:
+    ends = (depth + BLOCK, depth + 2 * BLOCK, depth + 3 * BLOCK)
+    places = []
+    for m in range(pairs):
+        for c in range(2):
+            lanes = pl.ds(c * BLOCK, BLOCK)
+            places.append((coupling.at[2 * m + c], cw.at[m, pl.ds(c * BLOCK, depth), lanes]))
+            if m in own_pairs:
+                rows = pl.ds(ends[c], BLOCK)
+                places.append((entry.at[2 * m + c], cw.at[m, rows, lanes]))
+    pieces = [
+        pltpu.make_async_copy(src, dst, pair_sem.at[i])
+        for i, (src, dst) in enumerate(places)
+    ]
+    for load in loads + pieces:
         load.start()
 
-    barrier = pltpu.get_barrier_semaphore()
-    pl.semaphore_signal(barrier, inc=1, device_id=east, device_id_type=MESH)
-    pl.semaphore_signal(barrier, inc=1, device_id=west, device_id_type=MESH)
-
-    @pl.when(has_south)
-    def _():
-        pl.semaphore_signal(barrier, inc=1, device_id=south, device_id_type=MESH)
-
-    @pl.when(has_north)
-    def _():
-        pl.semaphore_signal(barrier, inc=1, device_id=north, device_id_type=MESH)
+    blank = jnp.zeros((BLOCK, BLOCK), cw.dtype)
+    for m in range(pairs):
+        cw[m, :BLOCK, BLOCK:] = blank
+        cw[m, depth : ends[0], :BLOCK] = blank
+        if m in own_pairs:
+            cw[m, ends[1] : ends[2], :BLOCK] = blank
+            cw[m, ends[0] : ends[1], BLOCK:] = blank
 
     def remote(t, src, dst, side, target):
         return pltpu.make_async_remote_copy(
@@ -167,14 +190,14 @@
     loads[2].wait()
     for b in range(blocks):
         r[b] = r0[:, b * BLOCK : (b + 1) * BLOCK]
-    loads[3].wait()
-    loads[4].wait()
+    for load in loads[3:] + pieces:
+        load.wait()
 
     even = lax.broadcasted_iota(jnp.int32, (members, BLOCK), 1) % 2 == 0
 
-    def couple(b):
-        linked = [r[(b + k) % blocks] for k in range(links)]
-        return dot(jnp.concatenate(linked, axis=1), cw[b])
+    def couple(m, extra):
+        linked = [r[(2 * m + k) % blocks] for k in range(links + 1)] + extra
+        return dot(jnp.concatenate(linked, axis=1), cw[m, : len(linked) * BLOCK])
 
     def finish(indices, activations):
         features = []
@@ -191,11 +214,10 @@
     @pl.loop(0, STEPS)
     def _(t):
         own = [send[t, c] for c in range(2)]
-        for b in range(blocks):
-            total = couple(b)
-            if b in own_blocks:
-                total += dot(own[b % 2], iw[b])
-            acc[b] = total
+        for m in range(pairs):
+            total = couple(m, own if m in own_pairs else [])
+            acc[2 * m] = total[:, :BLOCK]
+            acc[2 * m + 1] = total[:, BLOCK:]
 
         result = finish(own_blocks, [acc[b] for b in own_blocks])
 
@@ -272,7 +294,7 @@
             pltpu.VMEM((members, features), f32),
             pltpu.VMEM((members, nodes), bf16),
             pltpu.VMEM((blocks, members, BLOCK), bf16),
-            pltpu.VMEM((blocks, links * BLOCK, BLOCK), bf16),
+            pltpu.VMEM((blocks // 2, (links + 3) * BLOCK, 2 * BLOCK), bf16),
             pltpu.VMEM((blocks, BLOCK, BLOCK), bf16),
             pltpu.VMEM((blocks, BLOCK, features), bf16),
             pltpu.VMEM((ns_count, 2 * BLOCK, BLOCK), bf16),
@@ -283,7 +305,8 @@
             pltpu.VMEM((STEPS, members, features), f32),
             pltpu.SemaphoreType.DMA((STEPS, 4)),
             pltpu.SemaphoreType.DMA((STEPS, 4)),
-            pltpu.SemaphoreType.DMA((5,)),
+            pltpu.SemaphoreType.DMA((4,)),
+            pltpu.SemaphoreType.DMA((2 * blocks,)),
             pltpu.SemaphoreType.DMA((STEPS,)),
         ],
         compiler_params=pltpu.CompilerParams(

time: 45 us -> 45.3 us (level)
  no operation moved by 1% of the time
where the time goes in v3:
time: 45.3 us; the launch traced here: 45.1 us
  Pallas kernels  43.2 us (95%)
  local copies, waits for them, and re-layouts  1.87 us (4%)
    pallas_call x1, Pallas kernels, per_device(): pl.pallas_call(functools.partial(kernel, n_lat, n_lon), out_shape=jax.Sha...  43.2 us
    unnamed x1, local copies, waits for them, and re-layouts  1.87 us

profile of v3, /device:TPU:0, one launch (start us, length us, event | category | flops | bytes accessed | tf_op | source)
XLA Modules:
  0.0 45.1 jit_solution(7987538415675890926)
XLA Ops:
  0.0 43.2 %shard_map.64 = f32[8,64,256]{2,1,0:T(8,128)} custom-call(s32[2,4]{1,0:T(2,128)} %bitcast.15, f32[64,256]{1,0:T(8,128)} %bitcast.14, bf16[64,2048]{1,0:T(8,128)(2,1)} %bitcast.13, bf16[16,512,128]{2,1,0:T(8,128)(2,1)} %bitcast.9, bf16[16,128,128]{2,1,0:T(8,128)(2,1)} %bitcast.12, bf16[16,128,256]{2,1,0:T(8,128)(2,1)} %bitcast.11), custom_call_target="tpu_custom_call" | custom-call | tf_op jit(solution)/shard_map/pallas_call | solution.py:288
  43.2 1.9 %copy.9 = f32[8,1,1,64,256]{4,3,2,1,0:T(8,128)} copy(f32[8,1,1,64,256]{4,3,2,1,0:T(8,128)} %bitcast.10) | data formatting | bytes 1048576

commit v4 on v2

--- a/solution.py
+++ b/solution.py
@@ -10,6 +10,7 @@
 VARS = 32
 OV = 4
 STEPS = 8
+PARTS = 2
 BLOCK = 128
 MESH = pl.DeviceIdType.MESH
 
@@ -55,6 +56,7 @@
     sector = lax.axis_index("lon")
     east = (band, lax.rem(sector + 1, n_lon))
     west = (band, lax.rem(sector + n_lon - 1, n_lon))
+    size = members // PARTS
     far = lax.rem(sector, 2)
     near = 1 - far
     south = (lax.rem(band + 1, n_lat), sector)
@@ -62,6 +64,18 @@
     has_north = band > 0
     has_south = band < n_lat - 1
 
+    barrier = pltpu.get_barrier_semaphore()
+    pl.semaphore_signal(barrier, inc=1, device_id=east, device_id_type=MESH)
+    pl.semaphore_signal(barrier, inc=1, device_id=west, device_id_type=MESH)
+
+    @pl.when(has_south)
+    def _():
+        pl.semaphore_signal(barrier, inc=1, device_id=south, device_id_type=MESH)
+
+    @pl.when(has_north)
+    def _():
+        pl.semaphore_signal(barrier, inc=1, device_id=north, device_id_type=MESH)
+
     loads = [
         pltpu.make_async_copy(src, dst, load_sem.at[i])
         for i, (src, dst) in enumerate(
@@ -71,41 +85,36 @@
     for load in loads:
         load.start()
 
-    barrier = pltpu.get_barrier_semaphore()
-    pl.semaphore_signal(barrier, inc=1, device_id=east, device_id_type=MESH)
-    pl.semaphore_signal(barrier, inc=1, device_id=west, device_id_type=MESH)
-
-    @pl.when(has_south)
-    def _():
-        pl.semaphore_signal(barrier, inc=1, device_id=south, device_id_type=MESH)
-
-    @pl.when(has_north)
-    def _():
-        pl.semaphore_signal(barrier, inc=1, device_id=north, device_id_type=MESH)
-
-    def remote(t, src, dst, side, target):
+    def remote(t, src, dst, slot, target):
         return pltpu.make_async_remote_copy(
             src_ref=src,
             dst_ref=dst,
-            send_sem=send_sem.at[t, side],
-            recv_sem=recv_sem.at[t, side],
+            send_sem=send_sem.at[t, slot],
+            recv_sem=recv_sem.at[t, slot],
             device_id=target,
             device_id_type=MESH,
         )
 
-    def to_lon(t, side):
+    def to_lon(t, side, part):
         target = (band, lax.rem(sector + 2 * side - 1 + n_lon, n_lon))
-        return remote(t, send.at[t, side], we_in.at[t, 1 - side], 1 - side, target)
+        rows = pl.ds(part * size, size)
+        return remote(
+            t,
+            send.at[t, side, rows],
+            we_in.at[t, 1 - side, rows],
+            2 + (1 - side) * PARTS + part,
+            target,
+        )
 
     def to_south(t):
-        return remote(t, send.at[t], ns_in.at[t, 0], 2, south)
+        return remote(t, send.at[t], ns_in.at[t, 0], 0, south)
 
     def to_north(t):
-        return remote(t, send.at[t], ns_in.at[t, 1], 3, north)
+        return remote(t, send.at[t], ns_in.at[t, 1], 1, north)
 
     def start_sends(t):
-        to_lon(t, far).start()
-        to_lon(t, near).start()
+        for part in range(PARTS):
+            to_lon(t, near, part).start()
 
         @pl.when(has_south)
         def _():
@@ -116,8 +125,9 @@
             to_north(t).start()
 
     def wait_sends(t):
-        to_lon(t, far).wait_send()
-        to_lon(t, near).wait_send()
+        for part in range(PARTS):
+            to_lon(t, far, part).wait_send()
+            to_lon(t, near, part).wait_send()
 
         @pl.when(has_south)
         def _():
@@ -127,19 +137,23 @@
         def _():
             to_north(t).wait_send()
 
-    def put_state(t, value):
+    def put_state(t, part, value):
         rounded = value.astype(jnp.bfloat16)
-        send[t, 0] = rounded[:, :BLOCK]
-        send[t, 1] = rounded[:, BLOCK:]
+        rows = slice(part * size, (part + 1) * size)
+        send[t, 0, rows] = rounded[:, :BLOCK]
+        send[t, 1, rows] = rounded[:, BLOCK:]
 
     def dot(a, b):
         return jnp.dot(a, b, preferred_element_type=jnp.float32)
 
     loads[0].wait()
-    put_state(0, u0[...])
+    for part in range(PARTS):
+        put_state(0, part, u0[part * size : (part + 1) * size, :])
     pl.semaphore_wait(
         barrier, 2 + has_north.astype(jnp.int32) + has_south.astype(jnp.int32)
     )
+    for part in range(PARTS):
+        to_lon(0, far, part).start()
     start_sends(0)
 
     @pl.when(jnp.logical_not(has_north))
@@ -170,17 +184,16 @@
     loads[3].wait()
     loads[4].wait()
 
-    even = lax.broadcasted_iota(jnp.int32, (members, BLOCK), 1) % 2 == 0
-
     def couple(b):
         linked = [r[(b + k) % blocks] for k in range(links)]
         return dot(jnp.concatenate(linked, axis=1), cw[b])
 
-    def finish(indices, activations):
+    def finish(indices, activations, rows=slice(None)):
+        even = lax.broadcasted_iota(jnp.int32, activations[0].shape, 1) % 2 == 0
         features = []
         for b, activation in zip(indices, activations):
             fresh = jnp.tanh(activation).astype(jnp.bfloat16)
-            r[b] = fresh
+            r[b, rows] = fresh
             wide = fresh.astype(jnp.float32)
             features.append(jnp.where(even, wide * wide, wide).astype(jnp.bfloat16))
         return dot(
@@ -223,26 +236,37 @@
             [acc[b] + dot(sides[b % 2], nsw[n]) for n, b in enumerate(ns_blocks)],
         )
 
-        for side in (near, far):
-            to_lon(t, 1 - side).wait_recv()
+        def finish_side(side, rows):
             indices = [2 * m + side for m in we_pairs]
             entered = dot(
-                we_in[t, side], jnp.concatenate([iw[b] for b in indices], axis=1)
+                we_in[t, side, rows], jnp.concatenate([iw[b] for b in indices], axis=1)
             )
-            result += finish(
-                indices,
-                [
-                    acc[b] + entered[:, n * BLOCK : (n + 1) * BLOCK]
-                    for n, b in enumerate(indices)
-                ],
-            )
+            activations = [
+                acc[b, rows] + entered[:, n * BLOCK : (n + 1) * BLOCK]
+                for n, b in enumerate(indices)
+            ]
+            return finish(indices, activations, rows)
+
+        for part in range(PARTS):
+            to_lon(t, 1 - near, part).wait_recv()
+        result += finish_side(near, slice(0, members))
+
+        for part in range(PARTS):
+            rows = slice(part * size, (part + 1) * size)
+            to_lon(t, 1 - far, part).wait_recv()
+            value = result[rows] + finish_side(far, rows)
+
+            @pl.when(t < STEPS - 1)
+            def _():
+                put_state(t + 1, part, value)
+                to_lon(t + 1, far, part).start()
+
+            outbuf[t, rows] = value
 
         @pl.when(t < STEPS - 1)
         def _():
-            put_state(t + 1, result)
             start_sends(t + 1)
 
-        outbuf[t] = result
         pltpu.make_async_copy(outbuf.at[t], out.at[t], out_sem.at[t]).start()
 
     last = STEPS - 1
@@ -281,8 +305,8 @@
             pltpu.VMEM((STEPS, 2, members, BLOCK), bf16),
             pltpu.VMEM((STEPS, 2, 2, members, BLOCK), bf16),
             pltpu.VMEM((STEPS, members, features), f32),
-            pltpu.SemaphoreType.DMA((STEPS, 4)),
-            pltpu.SemaphoreType.DMA((STEPS, 4)),
+            pltpu.SemaphoreType.DMA((STEPS, 2 + 2 * PARTS)),
+            pltpu.SemaphoreType.DMA((STEPS, 2 + 2 * PARTS)),
             pltpu.SemaphoreType.DMA((5,)),
             pltpu.SemaphoreType.DMA((STEPS,)),
         ],

time: 45 us -> 44.8 us (level)
  no operation moved by 1% of the time
where the time goes in v4:
time: 44.8 us; the launch traced here: 44.6 us
  Pallas kernels  42.7 us (95%)
  local copies, waits for them, and re-layouts  1.87 us (4%)
    pallas_call x1, Pallas kernels, per_device(): pl.pallas_call(functools.partial(kernel, n_lat, n_lon), out_shape=jax.Sha...  42.7 us
    unnamed x1, local copies, waits for them, and re-layouts  1.87 us

profile of v4, /device:TPU:0, one launch (start us, length us, event | category | flops | bytes accessed | tf_op | source)
XLA Modules:
  0.0 44.6 jit_solution(5798833584641119480)
XLA Ops:
  0.0 42.7 %shard_map.64 = f32[8,64,256]{2,1,0:T(8,128)} custom-call(s32[2,4]{1,0:T(2,128)} %bitcast.15, f32[64,256]{1,0:T(8,128)} %bitcast.14, bf16[64,2048]{1,0:T(8,128)(2,1)} %bitcast.13, bf16[16,512,128]{2,1,0:T(8,128)(2,1)} %bitcast.9, bf16[16,128,128]{2,1,0:T(8,128)(2,1)} %bitcast.12, bf16[16,128,256]{2,1,0:T(8,128)(2,1)} %bitcast.11), custom_call_target="tpu_custom_call" | custom-call | tf_op jit(solution)/shard_map/pallas_call | solution.py:290
  42.7 1.9 %copy.9 = f32[8,1,1,64,256]{4,3,2,1,0:T(8,128)} copy(f32[8,1,1,64,256]{4,3,2,1,0:T(8,128)} %bitcast.10) | data formatting | bytes 1048576

commit v5 on v4

--- a/solution.py
+++ b/solution.py
@@ -311,9 +311,15 @@
             pltpu.SemaphoreType.DMA((STEPS,)),
         ],
         compiler_params=pltpu.CompilerParams(
-            collective_id=0, has_side_effects=True, vmem_limit_bytes=63 * 1024 * 1024
+            collective_id=0, has_side_effects=True, vmem_limit_bytes=24 * 1024 * 1024
         ),
-    )(lists, state, reservoir, weights, entry, read)
+    )(
+        lists,
+        *(
+            pltpu.with_memory_space_constraint(x, pltpu.MemorySpace.HBM)
+            for x in (state, reservoir, weights, entry, read)
+        ),
+    )
     return forecast[:, None, None]
 
 

time: 44.8 us -> 43.7 us (0.975)
  Pallas kernels: 42.7 us -> 42.1 us
    pallas_call x1, Pallas kernels: 42.7 us -> 42.1 us  [per_device(): pl.pallas_call(functools.partial(kernel, n_lat, n_lon), out_shape=jax.Sha...]
    unnamed x1 -> x3, local copies, waits for them, and re-layouts: 1.87 us -> 1.47 us
where the time goes in v5:
time: 43.7 us; the launch traced here: 43.6 us
  Pallas kernels  42.1 us (96%)
  local copies, waits for them, and re-layouts  1.47 us (3%)
    pallas_call x1, Pallas kernels, per_device(): pl.pallas_call(functools.partial(kernel, n_lat, n_lon), out_shape=jax.Sha...  42.1 us
    unnamed x3, local copies, waits for them, and re-layouts  1.47 us

profile of v5, /device:TPU:0, one launch (start us, length us, event | category | flops | bytes accessed | tf_op | source)
XLA Modules:
  0.0 43.6 jit_solution(3983773364514975853)
XLA Ops:
  0.0 0.0 copy-start
  0.0 0.7 %copy-done = s32[1,1,2,4]{3,2,1,0:T(2,128)S(1)} copy-done((s32[1,1,2,4]{3,2,1,0:T(2,128)S(1)}, s32[1,1,2,4]{3,2,1,0:T(2,128)}, u32[]{:S(2)}) %copy-start) | copy-done | bytes 56
  0.7 42.1 %shard_map.64 = f32[8,64,256]{2,1,0:T(8,128)S(1)} custom-call(s32[2,4]{1,0:T(2,128)S(1)} %bitcast.10, f32[64,256]{1,0:T(8,128)} %bitcast.15, bf16[64,2048]{1,0:T(8,128)(2,1)} %bitcast.14, bf16[16,512,128]{2,1,0:T(8,128)(2,1)} %bitcast.11, bf16[16,128,128]{2,1,0:T(8,128)(2,1)} %bitcast.13, bf16[16,128,256]{2,1,0:T(8,128)(2,1)} %bitcast.12), custom_call_target="tpu_custom_call" | custom-call | tf_op jit(solution)/shard_map/pallas_call | solution.py:290
  42.8 0.8 %copy.9 = f32[8,1,1,64,256]{4,3,2,1,0:T(8,128)} copy(f32[8,1,1,64,256]{4,3,2,1,0:T(8,128)S(1)} %bitcast.9) | data formatting | bytes 1048576
Async XLA Ops:
  0.0 0.7 %copy-start = (s32[1,1,2,4]{3,2,1,0:T(2,128)S(1)}, s32[1,1,2,4]{3,2,1,0:T(2,128)}, u32[]{:S(2)}) copy-start(s32[1,1,2,4]{3,2,1,0:T(2,128)} %param.11) | copy-start | bytes 100
